TPU v7x, 32 devices: a whole 2x2x4 slice. The times are simulated.
32 devices in a mesh: groups: 2 (over y), tile: 4 (over z), depth: 2 (over x), rep: 2 (over core).
Axes of the slice: x: 2, y: 2, z: 4, core: 2. Of those that a mesh axis runs over, the one named last changes fastest.
Arguments:
- cycle_integrals: float32 [10240, 32000], P(('groups', 'depth', 'rep'), 'tile'), parts along dimension 0, may hold values from -0.09375 to 0.09375
- amplitudes: float32 [5120, 32000], P('groups', 'tile'), parts along dimension 0, may hold values from -6 to 6
- occupied_irreps: int32 [160], P('groups'), parts along dimension 0, may hold values from 0 to 7
- virtual_irreps: int32 [1600], P('groups'), parts along dimension 0, may hold values from 0 to 7
Outputs:
- cycle_residual: float32 [5120, 5120], P(('groups', 'tile'), ('depth', 'rep')), parts along dimension 0
There are 2 independent parts, one for each index of `groups`. A program takes and returns all parts, laid end to end along the dimension named above; each array names one. Nothing has to cross between parts.
Inputs may be any that keep to these rules, and one draw needn't show every extreme that they name: `occupied_irreps`: D2h irrep labels; the product of two irreps is their exclusive or. `virtual_irreps`: D2h irrep labels; the product of two irreps is their exclusive or.
All inputs are finite; a program needn't handle non-finite values.
Results may differ from a plain program's by a relative error of at most 0.000071.
Values sent between devices are 32-bit elements; how exact they have to be, the bound alone decides.
A program may use at most 320 MiB of HBM per device.

v0:
```python
import functools

import jax
import jax.numpy as jnp
from jax import lax
from jax.experimental import pallas as pl
from jax.experimental.pallas import tpu as pltpu
from jax.sharding import PartitionSpec as P

BF16, F32 = jnp.bfloat16, jnp.float32
def split(x):
    high = x.astype(BF16)
    return high, (x - high.astype(F32)).astype(BF16)


def merge_kernel(slots, rank_ref, irow_ref, col_ref, i_ref, y_ref, pick_ref):
    @pl.when(pl.program_id(0) == 0)
    def _():
        slot = lax.broadcasted_iota(jnp.int32, pick_ref.shape, 0)
        pick_ref[...] = jnp.where(slot == rank_ref[...], 1.0, 0.0).astype(BF16)

    high, low = split(jnp.where(irow_ref[...] == col_ref[...], i_ref[...], 0.0))
    nt = (((1,), (1,)), ((), ()))
    y_ref[:slots] = lax.dot_general(pick_ref[...], high, nt, preferred_element_type=F32).astype(BF16)
    y_ref[slots:] = lax.dot_general(pick_ref[...], low, nt, preferred_element_type=F32).astype(BF16)


def merge(integrals_t, rank, irows, cols, slots):
    depth, n = integrals_t.shape
    kb = 512
    padded = cols.shape[0]
    whole = lambda s: (0, 0)
    return pl.pallas_call(
        functools.partial(merge_kernel, slots),
        grid=(padded // kb,),
        out_shape=jax.ShapeDtypeStruct((2 * slots, padded), BF16),
        in_specs=[
            pl.BlockSpec((1, n), whole),
            pl.BlockSpec((1, n), whole),
            pl.BlockSpec((kb, 1), lambda s: (s, 0)),
            pl.BlockSpec((kb, n), lambda s: (jnp.minimum(s, (depth - 1) // kb), 0)),
        ],
        out_specs=pl.BlockSpec((2 * slots, kb), lambda s: (0, s)),
        scratch_shapes=[pltpu.VMEM((slots, n), BF16)],
        compiler_params=pltpu.CompilerParams(vmem_limit_bytes=40 * 1024 * 1024),
        cost_estimate=pl.CostEstimate(
            flops=4 * n * slots * depth, bytes_accessed=4 * (n + slots) * depth, transcendentals=0
        ),
    )(rank[None, :], irows[None, :], cols[:, None], integrals_t)


def chunk_kernel(slots, dest_ref, arow_ref, col_ref, a_ref, y_ref, z_ref):
    @pl.when(pl.program_id(0) == 0)
    def _():
        z_ref[...] = jnp.zeros_like(z_ref)

    a_high, a_low = split(jnp.where(arow_ref[...] == col_ref[...], a_ref[...], 0.0))
    both = jnp.dot(y_ref[...], a_high, preferred_element_type=F32)
    rest = jnp.dot(y_ref[:slots], a_low, preferred_element_type=F32)
    z_ref[...] += both[:slots] + both[slots:] + rest


def chunk(dest, amplitudes_t, y, arows, cols, width):
    depth, m = amplitudes_t.shape
    slots = y.shape[0] // 2
    kb = 1024 if width <= 1280 else 512
    return pl.pallas_call(
        functools.partial(chunk_kernel, slots),
        grid_spec=pltpu.PrefetchScalarGridSpec(
            num_scalar_prefetch=1,
            grid=(pl.cdiv(depth, kb),),
            in_specs=[
                pl.BlockSpec((1, width), lambda s, d: (0, d[0])),
                pl.BlockSpec((kb, 1), lambda s, d: (s, 0)),
                pl.BlockSpec((kb, width), lambda s, d: (s, d[0])),
                pl.BlockSpec((2 * slots, kb), lambda s, d: (0, s)),
            ],
            out_specs=pl.BlockSpec((slots, width), lambda s, d: (0, 0)),
        ),
        out_shape=jax.ShapeDtypeStruct((slots, width), F32),
        compiler_params=pltpu.CompilerParams(vmem_limit_bytes=52 * 1024 * 1024),
        cost_estimate=pl.CostEstimate(
            flops=6 * width * slots * depth, bytes_accessed=4 * (width + slots) * depth, transcendentals=0
        ),
    )(dest, arows[None, :], cols[:, None], amplitudes_t, y)


def expand_kernel(slots, rank_ref, icol_ref, row_ref, *refs):
    out_ref = refs[-1]
    slot = lax.broadcasted_iota(jnp.int32, (slots, rank_ref.shape[1]), 0)
    pick = jnp.where(slot == rank_ref[...], 1.0, 0.0).astype(BF16)
    total = refs[0][...]
    for z_ref in refs[1:-1]:
        total += z_ref[...]
    high, low = split(total.T)
    full = jnp.dot(high, pick, preferred_element_type=F32) + jnp.dot(low, pick, preferred_element_type=F32)
    out_ref[...] = jnp.where(row_ref[...] == icol_ref[...], full, 0.0)


def expand(terms, rank, irows, kept):
    slots, m = terms[0].shape
    n = rank.shape[0]
    block = 128 if m % 128 == 0 else m
    whole = lambda s: (0, 0)
    return pl.pallas_call(
        functools.partial(expand_kernel, slots),
        grid=(m // block,),
        out_shape=jax.ShapeDtypeStruct((m, n), F32),
        in_specs=[
            pl.BlockSpec((1, n), whole),
            pl.BlockSpec((1, n), whole),
            pl.BlockSpec((block, 1), lambda s: (s, 0)),
        ]
        + [pl.BlockSpec((slots, block), lambda s: (0, s))] * len(terms),
        out_specs=pl.BlockSpec((block, n), lambda s: (s, 0)),
        compiler_params=pltpu.CompilerParams(vmem_limit_bytes=32 * 1024 * 1024),
    )(rank[None, :], irows[None, :], kept[:, None], *terms)


def local(cycle_integrals, amplitudes, occupied_irreps, virtual_irreps):
    n, depth = cycle_integrals.shape
    m = amplitudes.shape[0]
    tiles = lax.axis_size("tile")
    occ = occupied_irreps.shape[0]
    reps = lax.axis_size("depth") * lax.axis_size("rep")
    used = -(-max(tiles * depth, m, reps * n) // occ)
    pair_irreps = jnp.bitwise_xor(virtual_irreps[:used, None], occupied_irreps[None, :]).reshape(-1)
    me = lax.axis_index("tile")
    cols = lax.dynamic_slice_in_dim(pair_irreps, me * depth, depth)
    cols = jnp.pad(cols, (0, -depth % 1024), constant_values=-1)
    row_start = (lax.axis_index("depth") * lax.axis_size("rep") + lax.axis_index("rep")) * n
    irows = lax.dynamic_slice_in_dim(pair_irreps, row_start, n)
    arows = pair_irreps[:m]
    kept_rows = m // tiles
    kept = lax.dynamic_slice_in_dim(arows, me * kept_rows, kept_rows)

    at = jnp.arange(n, dtype=jnp.int32)
    earlier = (irows[:, None] == irows[None, :]) & (at[:, None] < at[None, :])
    rank = jnp.sum(earlier.astype(jnp.int32), axis=0)
    slots = -(-3 * n // 1280) * 128

    every = pair_irreps[: reps * n].reshape(1, reps, n)
    counts = jnp.sum((every == jnp.arange(8, dtype=jnp.int32)[:, None, None]).astype(jnp.int32), axis=2)
    mine = jnp.broadcast_to(jnp.max(counts), (8, 128))
    most = mine
    groups = lax.axis_size("groups")
    for shift in range(1, groups):
        other = lax.ppermute(mine, "groups", [(g, (g + shift) % groups) for g in range(groups)])
        most = jnp.maximum(most, other)
    rounds = (most[0, 0] + slots - 1) // slots

    integrals_t, amplitudes_t = cycle_integrals.T, amplitudes.T

    def one_round(base):
        moved = rank - base
        y = merge(integrals_t, moved, irows, cols, slots)
        if tiles > 4 or kept_rows % 128:
            z = chunk(jnp.zeros((1,), jnp.int32), amplitudes_t, y, arows, cols, m)
            terms = [lax.psum_scatter(z, "tile", scatter_dimension=1, tiled=True)]
        else:
            terms, last = [], None
            far = sorted(range(1, tiles), key=lambda s: abs(2 * s - tiles))
            for shift in far + [0]:
                dest = lax.rem(me + shift, tiles).astype(jnp.int32).reshape(1)
                if last is not None:
                    dest, _ = lax.optimization_barrier((dest, last))
                last = chunk(dest, amplitudes_t, y, arows, cols, kept_rows)
                if shift:
                    terms.append(lax.ppermute(last, "tile", [(t, (t + shift) % tiles) for t in range(tiles)]))
                else:
                    terms.append(last)
        return expand(terms, moved, irows, kept)

    out = one_round(0)

    def more(state):
        r, total = state
        return r + 1, total + one_round(r * slots)

    return lax.while_loop(lambda s: s[0] < rounds, more, (jnp.int32(1), out))[1]


def solution(mesh):
    return jax.shard_map(
        local,
        mesh=mesh,
        in_specs=(
            P(("groups", "depth", "rep"), "tile"),
            P("groups", "tile"),
            P("groups"),
            P("groups"),
        ),
        out_specs=P(("groups", "tile"), ("depth", "rep")),
        check_vma=False,
    )
```

profile of v0, /device:TPU:0, one launch (start us, length us, event | category | flops | bytes accessed | tf_op | source)
XLA Modules:
  0.0 155.0 jit_solution(16346723288686028495)
XLA Ops:
  0.0 0.7 slice.16
  0.7 0.8 broadcast_xor_fusion
  1.5 0.2 xor.20
  1.6 0.1 dynamic_slice.9
  1.7 0.0 copy-start.6
  1.7 0.6 convert_reduce_fusion
  2.3 0.1 dynamic_slice.11
  2.4 2.6 %copy.24.col_ref = s32[8192,1]{1,0:T(8,128)} copy(s32[8192,1]{0,1:T(1,128)S(1)} %bitcast.29) | data formatting | bytes 65536 | tf_op jit(solution)/shard_map/broadcast_in_dim | solution.py:85
  5.1 0.1 broadcast_in_dim.23.arow_ref
  5.1 0.0 copy-start.1
  5.2 2.2 %copy-done.1 = s32[8192,1]{1,0:T(8,128)S(1)} copy-done((s32[8192,1]{1,0:T(8,128)S(1)}, s32[8192,1]{1,0:T(8,128)}, u32[]{:S(2)}) %copy-start.1) | copy-done | bytes 32792
  7.3 30.5 %shard_map.46.y_ref = bf16[768,8192]{1,0:T(8,128)(2,1)} custom-call(s32[1,1280]{1,0:T(1,128)S(1)} %broadcast_in_dim.20.rank_ref, s32[1,1280]{1,0:T(1,128)S(1)} %broadcast_in_dim.21.irow_ref.icol_ref, s32[8192,1]{1,0:T(8,128)S(1)} %copy-done.1, f32[8000,1280]{1,0:T(8,128)} %bitcast.31), custom_call_target="tpu_custom_call" | custom-call | flops 15728640000 | bytes 53248000 | tf_op jit(solution)/shard_map/pallas_call | solution.py:33
  37.9 21.7 %shard_map.47 = f32[384,640]{1,0:T(8,128)} custom-call(s32[1]{0:T(128)} %bitcast.5.dest_ref, s32[1,2560]{1,0:T(1,128)S(1)} %broadcast_in_dim.23.arow_ref, s32[8192,1]{1,0:T(8,128)} %copy.24.col_ref, f32[8000,2560]{1,0:T(8,128)} %bitcast.7.a_ref, bf16[768,8192]{1,0:T(8,128)(2,1)} %shard_map.46.y_ref), custom_call_target="tpu_custom_call" | custom-call | flops 11796480000 | bytes 32768000 | tf_op jit(solution)/shard_map/pallas_call | solution.py:67
  59.5 4.1 %collective-permute-start.3 = (f32[384,640]{1,0:T(8,128)}, f32[384,640]{1,0:T(8,128)S(1)}, u32[]{:S(2)}, u32[]{:S(2)}) collective-permute-start(f32[384,640]{1,0:T(8,128)} %shard_map.47), channel_id=1, source_target_pairs={{0,8},{4,12},{8,0},{12,4},{1,9},{5,13},{9,1},{13,5},{2,10},{6,14},... | collective-permute-start | bytes 2949128 | tf_op jit(solution)/shard_map/ppermute | solution.py:169
  63.6 21.7 %shard_map.48 = f32[384,640]{1,0:T(8,128)} custom-call(s32[1]{0:T(128)} %bitcast.9.dest_ref, s32[1,2560]{1,0:T(1,128)S(1)} %broadcast_in_dim.23.arow_ref, s32[8192,1]{1,0:T(8,128)} %copy.24.col_ref, f32[8000,2560]{1,0:T(8,128)} %bitcast.7.a_ref, bf16[768,8192]{1,0:T(8,128)(2,1)} %shard_map.46.y_ref), custom_call_target="tpu_custom_call" | custom-call | flops 11796480000 | bytes 32768000 | tf_op jit(solution)/shard_map/pallas_call | solution.py:67
  85.3 1.6 %collective-permute-start.4 = (f32[384,640]{1,0:T(8,128)}, f32[384,640]{1,0:T(8,128)S(1)}, u32[]{:S(2)}, u32[]{:S(2)}) collective-permute-start(f32[384,640]{1,0:T(8,128)} %shard_map.48), channel_id=1, source_target_pairs={{0,4},{4,8},{8,12},{12,0},{1,5},{5,9},{9,13},{13,1},{2,6},{6,10},{... | collective-permute-start | bytes 2949128 | tf_op jit(solution)/shard_map/ppermute | solution.py:169
  86.8 21.7 %shard_map.49 = f32[384,640]{1,0:T(8,128)} custom-call(s32[1]{0:T(128)} %bitcast.10.dest_ref, s32[1,2560]{1,0:T(1,128)S(1)} %broadcast_in_dim.23.arow_ref, s32[8192,1]{1,0:T(8,128)} %copy.24.col_ref, f32[8000,2560]{1,0:T(8,128)} %bitcast.7.a_ref, bf16[768,8192]{1,0:T(8,128)(2,1)} %shard_map.46.y_ref), custom_call_target="tpu_custom_call" | custom-call | flops 11796480000 | bytes 32768000 | tf_op jit(solution)/shard_map/pallas_call | solution.py:67
  108.5 2.3 %collective-permute-start.5 = (f32[384,640]{1,0:T(8,128)}, f32[384,640]{1,0:T(8,128)}, u32[]{:S(2)}, u32[]{:S(2)}) collective-permute-start(f32[384,640]{1,0:T(8,128)} %shard_map.49), channel_id=1, source_target_pairs={{0,12},{4,0},{8,4},{12,8},{1,13},{5,1},{9,5},{13,9},{2,14},{6,2},{... | collective-permute-start | bytes 2949128 | tf_op jit(solution)/shard_map/ppermute | solution.py:169
  110.8 0.1 eq.31
  110.9 0.2 convert_reduce_fusion.1
  111.1 0.6 reduce_max.9
  111.7 0.6 broadcast_in_dim.25
  112.3 1.6 %collective-permute-start.6 = (s32[8,128]{1,0:T(8,128)S(1)}, s32[8,128]{1,0:T(8,128)S(1)}, u32[]{:S(2)}, u32[]{:S(2)}) collective-permute-start(s32[8,128]{1,0:T(8,128)S(1)} %broadcast_in_dim.25), channel_id=1, source_target_pairs={{0,16},{16,0},{1,17},{17,1},{2,18},{18,2},{3,19},{19,3},{4,20},{20... | collective-permute-start | bytes 12296 | tf_op jit(solution)/shard_map/ppermute | solution.py:148
  113.9 20.8 %shard_map.50.refs_3_ = f32[384,640]{1,0:T(8,128)S(1)} custom-call(s32[1]{0:T(128)} %bitcast.11.dest_ref, s32[1,2560]{1,0:T(1,128)S(1)} %broadcast_in_dim.23.arow_ref, s32[8192,1]{1,0:T(8,128)} %copy.24.col_ref, f32[8000,2560]{1,0:T(8,128)} %bitcast.7.a_ref, bf16[768,8192]{1,0:T(8,128)(2,1)} %shard_map.46.y_ref), custom_call_target="tpu_custom_call" | custom-call | flops 11796480000 | bytes 32768000 | tf_op jit(solution)/shard_map/pallas_call | solution.py:67
  134.7 0.1 slice.18
  134.8 0.0 copy-done.6
  134.8 0.0 copy-start.7
  134.8 0.6 copy-done.7
  135.4 0.1 dynamic_slice.10
  135.5 0.0 copy-start.4
  135.5 0.6 copy-done.4
  136.0 0.1 broadcast_in_dim.27.row_ref
  136.2 0.0 copy-start.5
  136.2 0.0 collective-permute-done.6
  136.2 0.6 broadcast_maximum_fusion
  136.8 0.5 slice.20
  137.9 10.9 %collective-permute-done.5.refs_2_ = f32[384,640]{1,0:T(8,128)} collective-permute-done((f32[384,640]{1,0:T(8,128)}, f32[384,640]{1,0:T(8,128)}, u32[]{:S(2)}, u32[]{:S(2)}) %collective-permute-start.5) | collective-permute-done | bytes 983072 | tf_op jit(solution)/shard_map/ppermute | solution.py:169
  148.9 0.0 collective-permute-done.4.refs_1_
  148.9 0.0 collective-permute-done.3.refs_0_
  148.9 6.1 %shard_map.51 = f32[640,1280]{1,0:T(8,128)} custom-call(s32[1,1280]{1,0:T(1,128)S(1)} %broadcast_in_dim.20.rank_ref, s32[1,1280]{1,0:T(1,128)S(1)} %broadcast_in_dim.21.irow_ref.icol_ref, s32[640,1]{1,0:T(8,128)S(1)} %broadcast_in_dim.27.row_ref, f32[384,640]{1,0:T(8,128)S(1)} %collective-permute-done.3.refs_0_, ...), custom_call_target="tpu_custom_call" | custom-call | tf_op jit(solution)/shard_map/pallas_call | solution.py:105
  155.0 0.0 copy-done.5
  (8 shorter events, 0.0 us)
Async XLA Ops:
  1.7 133.1 %copy-start.6 = (s32[1280]{0:T(1024)}, s32[1280]{0:T(1024)S(1)}, u32[]{:S(2)}) copy-start(s32[1280]{0:T(1024)S(1)} %dynamic_slice.9) | copy-start | bytes 15364
  5.1 2.2 %copy-start.1 = (s32[8192,1]{1,0:T(8,128)S(1)}, s32[8192,1]{1,0:T(8,128)}, u32[]{:S(2)}) copy-start(s32[8192,1]{1,0:T(8,128)} %copy.24.col_ref) | copy-start | bytes 98308
  59.5 89.3 %collective-permute-start.3 = (f32[384,640]{1,0:T(8,128)}, f32[384,640]{1,0:T(8,128)S(1)}, u32[]{:S(2)}, u32[]{:S(2)}) collective-permute-start(f32[384,640]{1,0:T(8,128)} %shard_map.47), channel_id=1, source_target_pairs={{0,8},{4,12},{8,0},{12,4},{1,9},{5,13},{9,1},{13,5},{2,10},{6,14},... | collective-permute-start | bytes 2949128 | tf_op jit(solution)/shard_map/ppermute | solution.py:169
  85.3 63.6 %collective-permute-start.4 = (f32[384,640]{1,0:T(8,128)}, f32[384,640]{1,0:T(8,128)S(1)}, u32[]{:S(2)}, u32[]{:S(2)}) collective-permute-start(f32[384,640]{1,0:T(8,128)} %shard_map.48), channel_id=1, source_target_pairs={{0,4},{4,8},{8,12},{12,0},{1,5},{5,9},{9,13},{13,1},{2,6},{6,10},{... | collective-permute-start | bytes 2949128 | tf_op jit(solution)/shard_map/ppermute | solution.py:169
  108.5 40.3 %collective-permute-start.5 = (f32[384,640]{1,0:T(8,128)}, f32[384,640]{1,0:T(8,128)}, u32[]{:S(2)}, u32[]{:S(2)}) collective-permute-start(f32[384,640]{1,0:T(8,128)} %shard_map.49), channel_id=1, source_target_pairs={{0,12},{4,0},{8,4},{12,8},{1,13},{5,1},{9,5},{13,9},{2,14},{6,2},{... | collective-permute-start | bytes 2949128 | tf_op jit(solution)/shard_map/ppermute | solution.py:169
  112.3 23.9 %collective-permute-start.6 = (s32[8,128]{1,0:T(8,128)S(1)}, s32[8,128]{1,0:T(8,128)S(1)}, u32[]{:S(2)}, u32[]{:S(2)}) collective-permute-start(s32[8,128]{1,0:T(8,128)S(1)} %broadcast_in_dim.25), channel_id=1, source_target_pairs={{0,16},{16,0},{1,17},{17,1},{2,18},{18,2},{3,19},{19,3},{4,20},{20... | collective-permute-start | bytes 12296 | tf_op jit(solution)/shard_map/ppermute | solution.py:148
  134.8 0.6 copy-start.7
  135.5 0.6 copy-start.4
  136.2 18.8 %copy-start.5 = (s32[640]{0:T(1024)S(1)}, s32[640]{0:T(1024)}, u32[]{:S(2)}) copy-start(s32[640]{0:T(1024)} %copy-done.4) | copy-start | bytes 7684
where the time goes:
time: 156 us; the launch traced here: 155 us
  Pallas kernels  122 us (78%)
  waiting for transfers between devices  11 us (7%)
  starting transfers between devices  9.48 us (6%)
  local copies, waits for them, and re-layouts  8.57 us (5%)
  other arithmetic  2.73 us (2%)
    pallas_call x4, Pallas kernels, chunk(): pl.pallas_call(functools.partial(chunk_kernel, slots), grid_spec=pltpu.Pr...  85.9 us
    pallas_call x1, Pallas kernels, merge(): pl.pallas_call(functools.partial(merge_kernel, slots), grid=(padded // kb...  30.5 us
    ppermute x3, waiting for transfers between devices, one_round(): lax.ppermute(last, 'tile', [(t, (t + shift) % tiles) for t in range(tiles)])  10.9 us
    ppermute x3, starting transfers between devices, one_round(): lax.ppermute(last, 'tile', [(t, (t + shift) % tiles) for t in range(tiles)])  7.9 us
    pallas_call x1, Pallas kernels, expand(): pl.pallas_call(functools.partial(expand_kernel, slots), grid=(m // block,...  6.09 us
    unnamed x10, local copies, waits for them, and re-layouts  3.34 us
  transfers between devices with their start and end apart: 4, of which 1 were waited for; matrix products, arithmetic and copies ran while one was open for 2% of the time, Pallas kernels for 41%

commit v1 on v0

--- a/solution.py
+++ b/solution.py
@@ -16,13 +16,12 @@
 def merge_kernel(slots, rank_ref, irow_ref, col_ref, i_ref, y_ref, pick_ref):
     @pl.when(pl.program_id(0) == 0)
     def _():
-        slot = lax.broadcasted_iota(jnp.int32, pick_ref.shape, 0)
-        pick_ref[...] = jnp.where(slot == rank_ref[...], 1.0, 0.0).astype(BF16)
+        slot = lax.broadcasted_iota(jnp.int32, (slots, rank_ref.shape[1]), 0)
+        pick_ref[...] = jnp.where(slot == rank_ref[...], 1.0, 0.0).T.astype(BF16)
 
     high, low = split(jnp.where(irow_ref[...] == col_ref[...], i_ref[...], 0.0))
-    nt = (((1,), (1,)), ((), ()))
-    y_ref[:slots] = lax.dot_general(pick_ref[...], high, nt, preferred_element_type=F32).astype(BF16)
-    y_ref[slots:] = lax.dot_general(pick_ref[...], low, nt, preferred_element_type=F32).astype(BF16)
+    y_ref[:slots] = jnp.dot(high, pick_ref[...], preferred_element_type=F32).T.astype(BF16)
+    y_ref[slots:] = jnp.dot(low, pick_ref[...], preferred_element_type=F32).T.astype(BF16)
 
 
 def merge(integrals_t, rank, irows, cols, slots):
@@ -41,7 +40,7 @@
             pl.BlockSpec((kb, n), lambda s: (jnp.minimum(s, (depth - 1) // kb), 0)),
         ],
         out_specs=pl.BlockSpec((2 * slots, kb), lambda s: (0, s)),
-        scratch_shapes=[pltpu.VMEM((slots, n), BF16)],
+        scratch_shapes=[pltpu.VMEM((n, slots), BF16)],
         compiler_params=pltpu.CompilerParams(vmem_limit_bytes=40 * 1024 * 1024),
         cost_estimate=pl.CostEstimate(
             flops=4 * n * slots * depth, bytes_accessed=4 * (n + slots) * depth, transcendentals=0
@@ -154,21 +153,27 @@
     def one_round(base):
         moved = rank - base
         y = merge(integrals_t, moved, irows, cols, slots)
-        if tiles > 4 or kept_rows % 128:
+        if tiles != 4 or kept_rows % 128:
             z = chunk(jnp.zeros((1,), jnp.int32), amplitudes_t, y, arows, cols, m)
             terms = [lax.psum_scatter(z, "tile", scatter_dimension=1, tiled=True)]
         else:
-            terms, last = [], None
-            far = sorted(range(1, tiles), key=lambda s: abs(2 * s - tiles))
-            for shift in far + [0]:
-                dest = lax.rem(me + shift, tiles).astype(jnp.int32).reshape(1)
+            side, place = me // 2, me % 2
+            beside = [(t, t + 1 - 2 * (t % 2)) for t in range(4)]
+            across = [(t, (t + 2) % 4) for t in range(4)]
+            order = [(1 - side, 1 - place), (1 - side, place), (side, 1 - place), (side, place)]
+            parts, last = [], None
+            for to_side, to_place in order:
+                dest = (2 * to_side + to_place).astype(jnp.int32).reshape(1)
                 if last is not None:
                     dest, _ = lax.optimization_barrier((dest, last))
                 last = chunk(dest, amplitudes_t, y, arows, cols, kept_rows)
-                if shift:
-                    terms.append(lax.ppermute(last, "tile", [(t, (t + shift) % tiles) for t in range(tiles)]))
-                else:
-                    terms.append(last)
+                parts.append(last)
+            gathered = parts[1] + lax.ppermute(parts[0], "tile", beside)
+            terms = [
+                parts[3],
+                lax.ppermute(parts[2], "tile", beside),
+                lax.ppermute(gathered, "tile", across),
+            ]
         return expand(terms, moved, irows, kept)
 
     out = one_round(0)

time: 156 us -> 163 us (1.045)
  waiting for transfers between devices: 11 us -> 18.1 us
  other arithmetic: 2.73 us -> 5.17 us
  starting transfers between devices: 9.48 us -> 7.66 us
    ppermute x3, waiting for transfers between devices: 10.9 us -> 18.1 us  [the longest x1 10.7 us: one_round(): lax.ppermute(gathered, 'tile', across)]
    pallas_call x1, Pallas kernels: 30.5 us -> 33.5 us  [merge(): pl.pallas_call(functools.partial(merge_kernel, slots), grid=(padded // kb...]
    ppermute x3, starting transfers between devices: 7.9 us -> 5.64 us  [the longest x1 3.06 us: one_round(): gathered = parts[1] + lax.ppermute(parts[0], 'tile', beside)]
    add x0 -> x1, other arithmetic: none -> 2.25 us  [one_round(): gathered = parts[1] + lax.ppermute(parts[0], 'tile', beside)]
    pallas_call x4, Pallas kernels: 85.9 us -> 83.9 us  [chunk(): pl.pallas_call(functools.partial(chunk_kernel, slots), grid_spec=pltpu.Pr...]
  transfers between devices with their start and end apart: 4 -> 4, of which waited for: 1 -> 2; matrix products, arithmetic and copies ran while one was open for 2% -> 3% of each run, Pallas kernels for 41% -> 39%
where the time goes in v1:
time: 163 us
  Pallas kernels  122 us (75%)
  waiting for transfers between devices  18.1 us (11%)
  local copies, waits for them, and re-layouts  8.77 us (5%)
  starting transfers between devices  7.66 us (5%)
  other arithmetic  5.17 us (3%)
    pallas_call x4, Pallas kernels, chunk(): pl.pallas_call(functools.partial(chunk_kernel, slots), grid_spec=pltpu.Pr...  83.9 us
    pallas_call x1, Pallas kernels, merge(): pl.pallas_call(functools.partial(merge_kernel, slots), grid=(padded // kb...  33.5 us
    ppermute x1, waiting for transfers between devices, one_round(): lax.ppermute(gathered, 'tile', across)  10.7 us
    ppermute x1, waiting for transfers between devices, one_round(): lax.ppermute(parts[2], 'tile', beside)  7.45 us
    pallas_call x1, Pallas kernels, expand(): pl.pallas_call(functools.partial(expand_kernel, slots), grid=(m // block,...  4.56 us
    unnamed x10, local copies, waits for them, and re-layouts  3.34 us
  transfers between devices with their start and end apart: 4, of which 2 were waited for; matrix products, arithmetic and copies ran while one was open for 3% of the time, Pallas kernels for 39%

profile of v1, /device:TPU:0, one launch (start us, length us, event | category | flops | bytes accessed | tf_op | source)
XLA Modules:
  0.0 162.6 jit_solution(16029392835498876190)
XLA Ops:
  0.0 0.7 slice.16
  0.7 0.8 broadcast_xor_fusion
  1.5 0.2 xor.20
  1.6 0.1 dynamic_slice.9
  1.7 0.0 copy-start.6
  1.7 0.6 convert_reduce_fusion
  2.3 0.1 dynamic_slice.11
  2.4 2.6 %copy.24.col_ref = s32[8192,1]{1,0:T(8,128)} copy(s32[8192,1]{0,1:T(1,128)S(1)} %bitcast.29) | data formatting | bytes 65536 | tf_op jit(solution)/shard_map/broadcast_in_dim | solution.py:84
  5.1 0.1 broadcast_in_dim.23.arow_ref
  5.2 0.0 copy-start.1
  5.2 2.2 %copy-done.1 = s32[8192,1]{1,0:T(8,128)S(1)} copy-done((s32[8192,1]{1,0:T(8,128)S(1)}, s32[8192,1]{1,0:T(8,128)}, u32[]{:S(2)}) %copy-start.1) | copy-done | bytes 32792
  7.4 33.5 %shard_map.46.y_ref = bf16[768,8192]{1,0:T(8,128)(2,1)} custom-call(s32[1,1280]{1,0:T(1,128)S(1)} %broadcast_in_dim.20.rank_ref, s32[1,1280]{1,0:T(1,128)S(1)} %broadcast_in_dim.21.irow_ref.icol_ref, s32[8192,1]{1,0:T(8,128)S(1)} %copy-done.1, f32[8000,1280]{1,0:T(8,128)} %bitcast.31), custom_call_target="tpu_custom_call" | custom-call | flops 15728640000 | bytes 53248000 | tf_op jit(solution)/shard_map/pallas_call | solution.py:32
  40.9 20.8 %shard_map.47 = f32[384,640]{1,0:T(8,128)S(1)} custom-call(s32[1]{0:T(128)} %bitcast.8.dest_ref, s32[1,2560]{1,0:T(1,128)S(1)} %broadcast_in_dim.23.arow_ref, s32[8192,1]{1,0:T(8,128)} %copy.24.col_ref, f32[8000,2560]{1,0:T(8,128)} %bitcast.10.a_ref, bf16[768,8192]{1,0:T(8,128)(2,1)} %shard_map.46.y_ref), custom_call_target="tpu_custom_call" | custom-call | flops 11796480000 | bytes 32768000 | tf_op jit(solution)/shard_map/pallas_call | solution.py:66
  61.6 3.1 %collective-permute-start.4 = (f32[384,640]{1,0:T(8,128)S(1)}, f32[384,640]{1,0:T(8,128)}, u32[]{:S(2)}, u32[]{:S(2)}) collective-permute-start(f32[384,640]{1,0:T(8,128)S(1)} %shard_map.47), channel_id=1, source_target_pairs={{0,4},{4,0},{8,12},{12,8},{1,5},{5,1},{9,13},{13,9},{2,6},{6,2},{1... | collective-permute-start | bytes 2949128 | tf_op jit(solution)/shard_map/ppermute | solution.py:171
  64.7 20.7 %shard_map.48 = f32[384,640]{1,0:T(8,128)S(1)} custom-call(s32[1]{0:T(128)} %bitcast.7.dest_ref, s32[1,2560]{1,0:T(1,128)S(1)} %broadcast_in_dim.23.arow_ref, s32[8192,1]{1,0:T(8,128)} %copy.24.col_ref, f32[8000,2560]{1,0:T(8,128)} %bitcast.10.a_ref, bf16[768,8192]{1,0:T(8,128)(2,1)} %shard_map.46.y_ref), custom_call_target="tpu_custom_call" | custom-call | flops 11796480000 | bytes 32768000 | tf_op jit(solution)/shard_map/pallas_call | solution.py:66
  85.5 21.7 %shard_map.49 = f32[384,640]{1,0:T(8,128)} custom-call(s32[1]{0:T(128)} %bitcast.6.dest_ref, s32[1,2560]{1,0:T(1,128)S(1)} %broadcast_in_dim.23.arow_ref, s32[8192,1]{1,0:T(8,128)} %copy.24.col_ref, f32[8000,2560]{1,0:T(8,128)} %bitcast.10.a_ref, bf16[768,8192]{1,0:T(8,128)(2,1)} %shard_map.46.y_ref), custom_call_target="tpu_custom_call" | custom-call | flops 11796480000 | bytes 32768000 | tf_op jit(solution)/shard_map/pallas_call | solution.py:66
  107.1 0.1 collective-permute-start.3
  107.2 0.1 eq.37
  107.3 0.2 convert_reduce_fusion.1
  107.5 0.7 reduce_max.9
  108.2 0.7 broadcast_in_dim.25
  108.9 2.0 %collective-permute-start.6 = (s32[8,128]{1,0:T(8,128)S(1)}, s32[8,128]{1,0:T(8,128)S(1)}, u32[]{:S(2)}, u32[]{:S(2)}) collective-permute-start(s32[8,128]{1,0:T(8,128)S(1)} %broadcast_in_dim.25), channel_id=1, source_target_pairs={{0,16},{16,0},{1,17},{17,1},{2,18},{18,2},{3,19},{19,3},{4,20},{20... | collective-permute-start | bytes 12296 | tf_op jit(solution)/shard_map/ppermute | solution.py:147
  110.9 0.0 collective-permute-done.4
  110.9 2.3 %add.89 = f32[384,640]{1,0:T(8,128)} add(f32[384,640]{1,0:T(8,128)S(1)} %shard_map.48, f32[384,640]{1,0:T(8,128)} %collective-permute-done.4) | non-fusion elementwise | flops 245760 | bytes 2949120 | tf_op jit(solution)/shard_map/add | solution.py:171
  113.2 2.5 %collective-permute-start.5 = (f32[384,640]{1,0:T(8,128)}, f32[384,640]{1,0:T(8,128)S(1)}, u32[]{:S(2)}, u32[]{:S(2)}) collective-permute-start(f32[384,640]{1,0:T(8,128)} %add.89), channel_id=1, source_target_pairs={{0,8},{4,12},{8,0},{12,4},{1,9},{5,13},{9,1},{13,5},{2,10},{6,14},... | collective-permute-start | bytes 2949128 | tf_op jit(solution)/shard_map/ppermute | solution.py:175
  115.7 20.7 %shard_map.50.refs_0_ = f32[384,640]{1,0:T(8,128)S(1)} custom-call(s32[1]{0:T(128)} %bitcast.5.dest_ref, s32[1,2560]{1,0:T(1,128)S(1)} %broadcast_in_dim.23.arow_ref, s32[8192,1]{1,0:T(8,128)} %copy.24.col_ref, f32[8000,2560]{1,0:T(8,128)} %bitcast.10.a_ref, bf16[768,8192]{1,0:T(8,128)(2,1)} %shard_map.46.y_ref), custom_call_target="tpu_custom_call" | custom-call | flops 11796480000 | bytes 32768000 | tf_op jit(solution)/shard_map/pallas_call | solution.py:66
  136.4 0.1 slice.18
  136.5 0.0 copy-done.6
  136.5 0.0 copy-start.7
  136.5 0.6 copy-done.7
  137.1 0.1 dynamic_slice.10
  137.2 0.0 copy-start.4
  137.2 0.6 copy-done.4
  137.7 0.1 broadcast_in_dim.27.row_ref
  137.9 0.0 copy-start.5
  137.9 0.0 collective-permute-done.6
  137.9 0.7 broadcast_maximum_fusion
  138.6 0.6 slice.20
  139.9 7.5 %collective-permute-done.3.refs_1_ = f32[384,640]{1,0:T(8,128)S(1)} collective-permute-done((f32[384,640]{1,0:T(8,128)}, f32[384,640]{1,0:T(8,128)S(1)}, u32[]{:S(2)}, u32[]{:S(2)}) %collective-permute-start.3) | collective-permute-done | bytes 983072 | tf_op jit(solution)/shard_map/ppermute | solution.py:174
  147.4 10.7 %collective-permute-done.5.refs_2_ = f32[384,640]{1,0:T(8,128)S(1)} collective-permute-done((f32[384,640]{1,0:T(8,128)}, f32[384,640]{1,0:T(8,128)S(1)}, u32[]{:S(2)}, u32[]{:S(2)}) %collective-permute-start.5) | collective-permute-done | bytes 983072 | tf_op jit(solution)/shard_map/ppermute | solution.py:175
  158.0 4.6 %shard_map.51 = f32[640,1280]{1,0:T(8,128)} custom-call(s32[1,1280]{1,0:T(1,128)S(1)} %broadcast_in_dim.20.rank_ref, s32[1,1280]{1,0:T(1,128)S(1)} %broadcast_in_dim.21.irow_ref.icol_ref, s32[640,1]{1,0:T(8,128)S(1)} %broadcast_in_dim.27.row_ref, f32[384,640]{1,0:T(8,128)S(1)} %shard_map.50.refs_0_, f32[384,640]{1,0:T(8,128)S(1)} %collective-permute-done.3.refs_1_, ...), custom_call_target="tpu_custom_call" | custom-call | tf_op jit(solution)/shard_map/pallas_call | solution.py:104
  162.6 0.0 copy-done.5
  (8 shorter events, 0.0 us)
Async XLA Ops:
  1.7 134.8 %copy-start.6 = (s32[1280]{0:T(1024)}, s32[1280]{0:T(1024)S(1)}, u32[]{:S(2)}) copy-start(s32[1280]{0:T(1024)S(1)} %dynamic_slice.9) | copy-start | bytes 15364
  5.2 2.2 %copy-start.1 = (s32[8192,1]{1,0:T(8,128)S(1)}, s32[8192,1]{1,0:T(8,128)}, u32[]{:S(2)}) copy-start(s32[8192,1]{1,0:T(8,128)} %copy.24.col_ref) | copy-start | bytes 98308
  61.6 49.3 %collective-permute-start.4 = (f32[384,640]{1,0:T(8,128)S(1)}, f32[384,640]{1,0:T(8,128)}, u32[]{:S(2)}, u32[]{:S(2)}) collective-permute-start(f32[384,640]{1,0:T(8,128)S(1)} %shard_map.47), channel_id=1, source_target_pairs={{0,4},{4,0},{8,12},{12,8},{1,5},{5,1},{9,13},{13,9},{2,6},{6,2},{1... | collective-permute-start | bytes 2949128 | tf_op jit(solution)/shard_map/ppermute | solution.py:171
  107.1 40.2 %collective-permute-start.3 = (f32[384,640]{1,0:T(8,128)}, f32[384,640]{1,0:T(8,128)S(1)}, u32[]{:S(2)}, u32[]{:S(2)}) collective-permute-start(f32[384,640]{1,0:T(8,128)} %shard_map.49), channel_id=1, source_target_pairs={{0,4},{4,0},{8,12},{12,8},{1,5},{5,1},{9,13},{13,9},{2,6},{6,2},{1... | collective-permute-start | bytes 2949128 | tf_op jit(solution)/shard_map/ppermute | solution.py:174
  108.9 29.0 %collective-permute-start.6 = (s32[8,128]{1,0:T(8,128)S(1)}, s32[8,128]{1,0:T(8,128)S(1)}, u32[]{:S(2)}, u32[]{:S(2)}) collective-permute-start(s32[8,128]{1,0:T(8,128)S(1)} %broadcast_in_dim.25), channel_id=1, source_target_pairs={{0,16},{16,0},{1,17},{17,1},{2,18},{18,2},{3,19},{19,3},{4,20},{20... | collective-permute-start | bytes 12296 | tf_op jit(solution)/shard_map/ppermute | solution.py:147
  113.2 44.9 %collective-permute-start.5 = (f32[384,640]{1,0:T(8,128)}, f32[384,640]{1,0:T(8,128)S(1)}, u32[]{:S(2)}, u32[]{:S(2)}) collective-permute-start(f32[384,640]{1,0:T(8,128)} %add.89), channel_id=1, source_target_pairs={{0,8},{4,12},{8,0},{12,4},{1,9},{5,13},{9,1},{13,5},{2,10},{6,14},... | collective-permute-start | bytes 2949128 | tf_op jit(solution)/shard_map/ppermute | solution.py:175
  136.5 0.6 copy-start.7
  137.2 0.6 copy-start.4
  137.9 24.7 %copy-start.5 = (s32[640]{0:T(1024)S(1)}, s32[640]{0:T(1024)}, u32[]{:S(2)}) copy-start(s32[640]{0:T(1024)} %copy-done.4) | copy-start | bytes 7684
